TPU v7x, 128 devices: a whole 4x4x4 slice. The times are simulated.
128 devices in a mesh: box: 32 (over z, x, core), inc: 4 (over y).
Axes of the slice: x: 4, y: 4, z: 4, core: 2. Of those that a mesh axis runs over, the one named last changes fastest.
Arguments:
- leaves: float32 [1024, 2, 16, 2048], P('box', None, 'inc'), parts along dimension 2, may hold values from -6 to 6
- theta_a: float32 [32, 64], replicated, may hold values from -1 to 1
- phi_a: float32 [64, 128], replicated, may hold values from -0.75 to 0.75
- shift_b: float32 [8, 64, 128], replicated, may hold values from -3.140625 to 3.140625
- theta_b: float32 [64, 128], replicated, may hold values from -0.75 to 0.75
- phi_b: float32 [128, 256], replicated, may hold values from -0.5 to 0.5
- shift_c: float32 [8, 128, 256], replicated, may hold values from -3.140625 to 3.140625
- parent_map: int32 [128], replicated, may hold values from 0 to 15
- inter_list: int32 [128, 32], replicated, may hold values from 0 to 127
- op_index: int32 [128, 32], replicated, may hold values from 0 to 315
- trans_ops: float32 [2, 316, 64, 128], P(None, None, 'box'), may hold values from -0.75 to 0.75
Outputs:
- parents: float32 [16, 2, 16, 128, 256], P(None, None, 'inc', 'box'), parts along dimension 2
- incoming: float32 [128, 2, 16, 64, 128], P('box', None, 'inc'), parts along dimension 2
There are 4 independent parts, one for each index of `inc`. A program takes and returns all parts, laid end to end along the dimension named above; an argument that names none is the same for every part. Nothing has to cross between parts.
All inputs are finite; a program needn't handle non-finite values.
Results may differ from a plain program's by a relative error of at most 0.00007.
Values sent between devices are 32-bit elements; how exact they have to be, the bound alone decides.
A program may use at most 128 MiB of HBM per device.

v0:
```python
import functools

import jax
import jax.numpy as jnp
from jax import lax
from jax.experimental import pallas as pl
from jax.experimental.pallas import tpu as pltpu
from jax.sharding import PartitionSpec as P

F32 = jnp.float32
BF16 = jnp.bfloat16
MESH = pl.DeviceIdType.MESH
N = 32
NOPS = 316
LIST = 32
MERGE = 0.35

HOPS = (
    (2, 2),
    (2, 1), (2, 3), (1, 2), (3, 2),
    (0, 2), (2, 0),
    (1, 3), (3, 1),
    (1, 1), (3, 3),
    (0, 1), (0, 3), (1, 0), (3, 0),
)


def dot(a, b):
    return lax.dot_general(a, b, (((1,), (0,)), ((), ())), preferred_element_type=F32)


def dot_t(a, b):
    return lax.dot_general(a, b, (((0,), (0,)), ((), ())), preferred_element_type=F32)


def split(x):
    hi = x.astype(BF16)
    lo = (x - hi.astype(F32)).astype(BF16)
    return hi, lo


def split3(x):
    hi = x.astype(BF16)
    rest = x - hi.astype(F32)
    mid = rest.astype(BF16)
    lo = (rest - mid.astype(F32)).astype(BF16)
    return hi, mid, lo


def cos_sin(angle):
    h = angle * 0.5
    g = h * h
    s = 1.0 / 6227020800.0
    for c in (-1.0 / 39916800.0, 1.0 / 362880.0, -1.0 / 5040.0, 1.0 / 120.0, -1.0 / 6.0, 1.0):
        s = s * g + c
    s = s * h
    c0 = 1.0 / 479001600.0
    for c in (-1.0 / 3628800.0, 1.0 / 40320.0, -1.0 / 720.0, 1.0 / 24.0, -0.5, 1.0):
        c0 = c0 * g + c
    return 1.0 - 2.0 * s * s, 2.0 * s * c0


def iota(shape, dim):
    return lax.broadcasted_iota(jnp.int32, shape, dim)


def onehot(cond):
    return jnp.where(cond, 1.0, 0.0).astype(F32).astype(BF16)


def kernel(
    leaves_hbm, theta_a_hbm, phi_a_hbm, shift_b_hbm, theta_b_hbm, phi_b_hbm, shift_c_hbm,
    pmap_hbm, list_hbm, ops_hbm, trans_hbm,
    parents_ref, incoming_ref,
    leaves, theta_a, phi_a, shift_b, theta_b, phi_b, shift_c, pmap, ilist, iops, trans,
    q3, w3, v3, tab, acc, gains, cs,
    buf_a, recv_a, buf_b, recv_b, buf_c, recv_c, azi, group, total,
    in_sem, leaf_sem, send_a, got_a, send_b, got_b, send_c, got_c,
):
    me = lax.axis_index("box")
    z, x, core = me // 8, (me // 2) % 4, me % 2
    zs = [((z + k) % 4) * 8 for k in range(4)]
    xs = [((x + k) % 4) * 2 for k in range(4)]
    cores = [core, 1 - core]
    partners = [zs[dz] + xs[dx] + cores[dc] for dz, dx in HOPS for dc in range(2)]
    partners.append(zs[0] + xs[0] + cores[1])

    barrier = pltpu.get_barrier_semaphore()
    for d in partners:
        pl.semaphore_signal(barrier, inc=1, device_id={"box": d}, device_id_type=MESH)

    def fetch(k, src, dst):
        copy = pltpu.make_async_copy(src, dst, in_sem.at[k])
        copy.start()
        return copy

    get_theta_a = fetch(0, theta_a_hbm, theta_a)
    get_phi_a = fetch(1, phi_a_hbm, phi_a)
    get_leaves = []
    for q in range(4):
        copy = pltpu.make_async_copy(
            leaves_hbm.at[pl.ds(8 * q, 8)], leaves.at[pl.ds(8 * q, 8)], leaf_sem.at[q]
        )
        copy.start()
        get_leaves.append(copy)
    get_shift_b = fetch(2, shift_b_hbm, shift_b)
    get_theta_b = fetch(3, theta_b_hbm, theta_b)
    get_trans = fetch(4, trans_hbm, trans)
    get_list = fetch(5, list_hbm, ilist)
    get_ops = fetch(6, ops_hbm, iops)
    get_phi_b = fetch(7, phi_b_hbm, phi_b)
    get_pmap = fetch(8, pmap_hbm, pmap)
    get_shift_c = fetch(
        9, shift_c_hbm.at[:, pl.ds(pl.multiple_of(8 * (me // 2), 8), 8), :], shift_c
    )

    get_phi_a.wait()
    for i, half in enumerate(split(phi_a[...])):
        none = jnp.zeros_like(half)
        both = jnp.concatenate(
            [jnp.concatenate([half, none], 1), jnp.concatenate([none, half], 1)], 0
        )
        if i == 0:
            q3[0:128, :] = both
            q3[128:256, :] = both
        else:
            q3[256:384, :] = both

    get_theta_a.wait()
    col = iota((32, 128), 1)
    pick_t = onehot(iota((32, 128), 0) == 2 * ((col % 64) // 4) + col // 64)
    rep_u = onehot(iota((256, 64), 1) == iota((256, 64), 0) // 4)
    same = iota((256, 128), 0) % 4 == iota((256, 128), 1) % 4
    for i, half in enumerate(split(theta_a[...])):
        wide = dot(rep_u, dot_t(half, pick_t).astype(BF16))
        wide = jnp.where(same, wide, 0.0).astype(BF16)
        if i == 0:
            w3[:, 0:128] = wide
            w3[:, 256:384] = wide
        else:
            w3[:, 128:256] = wide

    get_shift_b.wait()
    rep_u3 = jnp.concatenate([rep_u, rep_u, rep_u], 1)

    @pl.loop(0, 8)
    def _(o):
        cosine, sine = cos_sin(shift_b[o])
        pair = MERGE * jnp.concatenate([cosine, sine], 1)
        tab[o] = dot(rep_u3, jnp.concatenate(split3(pair), 0))

    get_theta_b.wait()
    pick_u = onehot(iota((64, 256), 0) == iota((64, 256), 1) // 4)
    row = iota((512, 128), 0)
    rep_u2 = onehot(iota((512, 128), 1) == 4 * (row // 16) + row % 4)
    same = (iota((512, 256), 0) % 16) // 4 == iota((512, 256), 1) % 4
    for i, half in enumerate(split(theta_b[...])):
        wide = dot(rep_u2, dot_t(half, pick_u).astype(BF16))
        wide = jnp.where(same, wide, 0.0).astype(BF16)
        if i == 0:
            v3[:, 0:256] = wide
            v3[:, 512:768] = wide
        else:
            v3[:, 256:512] = wide

    def compute(q):
        def one_leaf(o, carry):
            pattern = leaves[8 * q + o].reshape(128, 128)
            hi, lo = split(pattern)
            y = dot(jnp.concatenate([hi, lo, hi], 1), q3[...])
            y = jnp.concatenate(
                [
                    jnp.concatenate([y[0:64, 0:128], y[64:128, 0:128]], 1),
                    jnp.concatenate([y[0:64, 128:256], y[64:128, 128:256]], 1),
                ],
                0,
            )
            hi, lo = split(y)
            up = dot(w3[...], jnp.concatenate([hi, hi, lo], 0))
            cosine, sine = tab[o, :, 0:128], tab[o, :, 128:256]
            re, im = up[:, 0:128], up[:, 128:256]
            turned = jnp.concatenate([cosine * re - sine * im, sine * re + cosine * im], 1)
            acc[...] += turned
            return carry

        acc[...] = jnp.zeros_like(acc)
        lax.fori_loop(0, 8, one_leaf, 0)
        middle = acc[...]
        for c in range(2):
            buf_a[q, :, c] = middle[:, 128 * c : 128 * c + 128].reshape(32, 8, 128)
        hi, lo = split(middle)
        polar = dot(v3[...], jnp.concatenate([hi, hi, lo], 0))
        for c in range(2):
            buf_b[q, :, c] = polar[:, 128 * c : 128 * c + 128].reshape(32, 16, 128)
        recv_a[4 * me + q] = buf_a[q, me]
        recv_b[4 * me + q] = buf_b[q, me]

    def send(q):
        for buf, recv, send_sem, got_sem in (
            (buf_a, recv_a, send_a, got_a),
            (buf_b, recv_b, send_b, got_b),
        ):
            for d in partners:
                pltpu.make_async_remote_copy(
                    src_ref=buf.at[q, d],
                    dst_ref=recv.at[4 * me + q],
                    send_sem=send_sem,
                    recv_sem=got_sem,
                    device_id={"box": d},
                    device_id_type=MESH,
                ).start()

    get_leaves[0].wait()
    compute(0)
    pl.semaphore_wait(barrier, N - 1)
    send(0)
    for q in range(1, 4):
        get_leaves[q].wait()

    @pl.loop(1, 4)
    def _(q):
        compute(q)
        send(q)

    get_trans.wait()
    upper = iota((8, 128), 0) < 4

    @pl.loop(0, NOPS // 4)
    def _(k):
        for j in range(4):
            for c in range(2):
                two = trans[c, 4 * k + j]
                gains[4 * k + j, c] = jnp.where(
                    upper,
                    jnp.broadcast_to(two[0:1], (8, 128)),
                    jnp.broadcast_to(two[1:2], (8, 128)),
                )

    def every(ref, send_sem, got_sem):
        return pltpu.make_async_remote_copy(
            src_ref=ref,
            dst_ref=ref,
            send_sem=send_sem,
            recv_sem=got_sem,
            device_id={"box": partners[-1]},
            device_id_type=MESH,
        )

    all_a = every(recv_a.at[pl.ds(0, 124)], send_a, got_a)
    all_b = every(recv_b.at[pl.ds(0, 124)], send_b, got_b)
    all_c = every(recv_c.at[:, :, pl.ds(0, 248), :], send_c, got_c)
    get_list.wait()
    get_ops.wait()
    all_a.wait_recv()

    def translate(d, put):
        @pl.loop(0, 4)
        def _(k):
            t = 4 * d + k
            sums = [jnp.zeros((8, 128), F32) for _ in range(4)]
            for j in range(LIST):
                s, o = ilist[j, t], iops[j, t]
                sr, si = recv_a[s, 0], recv_a[s, 1]
                gr, gi = gains[o, 0], gains[o, 1]
                sums[0] += gr * sr
                sums[1] += gi * si
                sums[2] += gr * si
                sums[3] += gi * sr
            put(k, sums[0] - sums[1], sums[2] + sums[3])

    for d in partners:

        def put(k, re, im, d=d):
            buf_c[d, k, 0] = re
            buf_c[d, k, 1] = im

        translate(d, put)
        pltpu.make_async_remote_copy(
            src_ref=buf_c.at[d],
            dst_ref=recv_c.at[:, :, pl.ds(pl.multiple_of(8 * me, 8), 8), :],
            send_sem=send_c,
            recv_sem=got_c,
            device_id={"box": d},
            device_id_type=MESH,
        ).start()

    def put_own(k, re, im):
        recv_c[k, 0, pl.ds(pl.multiple_of(8 * me, 8), 8), :] = re
        recv_c[k, 1, pl.ds(pl.multiple_of(8 * me, 8), 8), :] = im

    translate(me, put_own)

    get_phi_b.wait()
    hi, lo = split(phi_b[...])
    azi[0:128, :] = hi
    azi[128:256, :] = hi
    azi[256:384, :] = lo
    get_shift_c.wait()
    upper_half = core == 0
    for o in range(8):
        pair = MERGE * jnp.concatenate(cos_sin(shift_c[o]), 1)
        four = jnp.where(upper_half, pair[0:4], pair[4:8])
        cs[o] = jnp.concatenate([four] * 4, 0)
    get_pmap.wait()
    owner = onehot(iota((16, 128), 0) == pmap[...])
    rep_p = onehot(iota((256, 16), 1) == iota((256, 16), 0) // 16)
    owner_rows = dot(rep_p, owner).astype(BF16)
    same = iota((256, 256), 0) % 16 == iota((256, 256), 1) % 16
    box = iota((128, 256), 0)
    slot = iota((128, 256), 1) // 16
    total[...] = jnp.zeros_like(total)
    all_b.wait_recv()

    @pl.loop(0, 8)
    def _(o):
        pick_box = onehot(box == 8 * slot + o)
        pick = jnp.where(same, dot(owner_rows, pick_box), 0.0).astype(BF16)
        rows = [
            jnp.concatenate([recv_b[8 * m + o, 0], recv_b[8 * m + o, 1]], 1) for m in range(16)
        ]
        hi, lo = split(jnp.concatenate(rows, 0))
        merged = dot(jnp.concatenate([pick, pick], 1), jnp.concatenate([hi, lo], 0))
        cosine, sine = cs[o, :, 0:256], cs[o, :, 256:512]
        group[0:256, :] = merged[:, 0:128]
        group[256:512, :] = merged[:, 128:256]
        for h in range(2):
            parts = []
            for c in range(2):
                hi, lo = split(group[256 * c + 128 * h : 256 * c + 128 * h + 128, :])
                parts.append(
                    dot(jnp.concatenate([hi, lo, hi], 1), azi[...]).reshape(8, 16, 256)
                )
            re, im = parts
            for c, turned in enumerate(
                (cosine * re - sine * im, sine * re + cosine * im)
            ):
                total[pl.ds(8 * h, 8), c] += turned

    for i in range(4):
        parents_ref[:, :, i] = total[:, :, 4 * i : 4 * i + 4, :]

    all_c.wait_recv()
    for k in range(4):
        for c in range(2):
            for i in range(4):
                incoming_ref[k, c, i] = recv_c[k, c, pl.ds(i, 64, stride=4), :]
    all_a.wait_send()
    all_b.wait_send()
    all_c.wait_send()


def on_device(
    leaves, theta_a, phi_a, shift_b, theta_b, phi_b, shift_c, parent_map, inter_list, op_index,
    trans_ops,
):
    grid = leaves.reshape(32, 2, 4, 16, 128).transpose(0, 1, 3, 2, 4).reshape(32, 2, 64, 128)
    hbm = pl.BlockSpec(memory_space=pltpu.HBM)
    vmem = pl.BlockSpec(memory_space=pltpu.VMEM)

    def v(*shape, kind=F32):
        return pltpu.VMEM(shape, kind)

    dma = pltpu.SemaphoreType.DMA
    return pl.pallas_call(
        kernel,
        out_shape=(
            jax.ShapeDtypeStruct((16, 2, 4, 4, 256), F32),
            jax.ShapeDtypeStruct((4, 2, 4, 64, 128), F32),
        ),
        in_specs=[hbm] * 11,
        out_specs=(vmem, vmem),
        scratch_shapes=[
            v(32, 2, 64, 128), v(32, 64), v(64, 128), v(8, 64, 128), v(64, 128), v(128, 256),
            v(8, 8, 256), v(1, 128, kind=jnp.int32),
            pltpu.SMEM((LIST, 128), jnp.int32), pltpu.SMEM((LIST, 128), jnp.int32),
            v(2, NOPS, 2, 128),
            v(384, 256, kind=BF16), v(256, 384, kind=BF16), v(512, 768, kind=BF16),
            v(8, 256, 256), v(256, 256), v(NOPS, 2, 8, 128), v(8, 16, 512),
            v(4, 32, 2, 8, 128), v(128, 2, 8, 128),
            v(4, 32, 2, 16, 128), v(128, 2, 16, 128),
            v(32, 4, 2, 8, 128), v(4, 2, 256, 128),
            v(384, 256, kind=BF16), v(512, 128), v(16, 2, 16, 256),
            dma((10,)), dma((4,)), dma, dma, dma, dma, dma, dma,
        ],
        compiler_params=pltpu.CompilerParams(
            collective_id=0, has_side_effects=True, vmem_limit_bytes=48 * 2**20
        ),
    )(
        grid, theta_a, phi_a, shift_b, theta_b, phi_b, shift_c, parent_map.reshape(1, 128),
        inter_list.T, op_index.T, trans_ops,
    )


def solution(mesh):
    r = P()
    in_specs = (P("box", None, "inc", None),) + (r,) * 9 + (P(None, None, "box", None),)
    out_specs = (P(None, None, "inc", "box", None), P("box", None, "inc", None, None))
    return jax.shard_map(
        on_device, mesh=mesh, in_specs=in_specs, out_specs=out_specs, check_vma=False
    )
```

profile of v0, /device:TPU:1, one launch (start us, length us, event | category | flops | bytes accessed | tf_op | source)
XLA Modules:
  0.0 74.2 jit_solution(3158278303157284692)
XLA Ops:
  0.6 0.0 copy-start
  0.6 1.6 %copy-done = f32[32,2,4,2048]{3,2,1,0:T(4,128)S(1)} copy-done((f32[32,2,4,2048]{3,2,1,0:T(4,128)S(1)}, f32[32,2,4,2048]{3,2,1,0:T(4,128)}, u32[]{:S(2)}) %copy-start) | copy-done | bytes 2097176
  2.2 0.0 copy-start.1
  2.2 1.2 %copy-done.1 = f32[8,128,256]{2,1,0:T(8,128)S(1)} copy-done((f32[8,128,256]{2,1,0:T(8,128)S(1)}, f32[8,128,256]{2,1,0:T(8,128)}, u32[]{:S(2)}) %copy-start.1) | copy-done | bytes 1048600
  3.5 0.0 copy-start.2
  3.5 1.1 %copy-done.2 = f32[2,316,2,128]{3,2,1,0:T(2,128)S(1)} copy-done((f32[2,316,2,128]{3,2,1,0:T(2,128)S(1)}, f32[2,316,2,128]{3,2,1,0:T(2,128)}, u32[]{:S(2)}) %copy-start.2) | copy-done | bytes 647192
  4.5 0.0 copy-start.3
  4.5 0.9 %copy-done.3 = f32[8,64,128]{2,1,0:T(8,128)S(1)} copy-done((f32[8,64,128]{2,1,0:T(8,128)S(1)}, f32[8,64,128]{2,1,0:T(8,128)}, u32[]{:S(2)}) %copy-start.3) | copy-done | bytes 262168
  5.5 0.0 copy-start.4
  5.5 0.9 %copy-done.4 = f32[128,256]{1,0:T(8,128)S(1)} copy-done((f32[128,256]{1,0:T(8,128)S(1)}, f32[128,256]{1,0:T(8,128)}, u32[]{:S(2)}) %copy-start.4) | copy-done | bytes 131096
  6.4 0.0 copy-start.5
  6.4 0.8 %copy-done.5 = f32[64,128]{1,0:T(8,128)S(1)} copy-done((f32[64,128]{1,0:T(8,128)S(1)}, f32[64,128]{1,0:T(8,128)}, u32[]{:S(2)}) %copy-start.5) | copy-done | bytes 32792
  7.2 0.0 copy-start.6
  7.2 0.8 %copy-done.6 = f32[64,128]{1,0:T(8,128)S(1)} copy-done((f32[64,128]{1,0:T(8,128)S(1)}, f32[64,128]{1,0:T(8,128)}, u32[]{:S(2)}) %copy-start.6) | copy-done | bytes 32792
  7.9 0.0 copy-start.7
  7.9 0.7 copy-done.7
  8.6 0.0 copy-start.8
  8.6 0.7 copy-done.8
  9.3 0.0 copy-start.9
  9.3 0.7 copy-done.9
  10.1 0.0 copy-start.10
  10.1 0.7 copy-done.10
  10.7 61.7 %shard_map.122 = (f32[16,2,4,4,256]{4,3,2,1,0:T(4,128)S(1)}, f32[4,2,4,64,128]{4,3,2,1,0:T(8,128)S(1)}) custom-call(f32[32,2,64,128]{3,2,1,0:T(8,128)S(1)} %bitcast.8, f32[32,64]{1,0:T(8,128)S(1)} %copy-done.7, f32[64,128]{1,0:T(8,128)S(1)} %copy-done.5, f32[8,64,128]{2,1,0:T(8,128)S(1)} %copy-done.3, f32[64,128]{1,0:T(8,128)S(1)} %copy-done.6, ...), custom_call_target="tpu_custom_call" | custom-call | tf_op jit(solution)/shard_map/pallas_call | solution.py:364
  72.4 0.8 %copy.16 = f32[16,2,4,4,256]{4,3,2,1,0:T(4,128)} copy(f32[16,2,4,4,256]{4,3,2,1,0:T(4,128)S(1)} %get-tuple-element.4) | data formatting | bytes 1048576
  73.2 1.0 %copy.17 = f32[4,2,4,64,128]{4,3,2,1,0:T(8,128)} copy(f32[4,2,4,64,128]{4,3,2,1,0:T(8,128)S(1)} %get-tuple-element.5) | data formatting | bytes 2097152
Async XLA Ops:
  0.6 1.6 %copy-start = (f32[32,2,4,2048]{3,2,1,0:T(4,128)S(1)}, f32[32,2,4,2048]{3,2,1,0:T(4,128)}, u32[]{:S(2)}) copy-start(f32[32,2,4,2048]{3,2,1,0:T(4,128)} %param.11) | copy-start | bytes 6291460
  2.2 1.2 %copy-start.1 = (f32[8,128,256]{2,1,0:T(8,128)S(1)}, f32[8,128,256]{2,1,0:T(8,128)}, u32[]{:S(2)}) copy-start(f32[8,128,256]{2,1,0:T(8,128)} %shift_c_hbm.1) | copy-start | bytes 3145732
  3.5 1.1 %copy-start.2 = (f32[2,316,2,128]{3,2,1,0:T(2,128)S(1)}, f32[2,316,2,128]{3,2,1,0:T(2,128)}, u32[]{:S(2)}) copy-start(f32[2,316,2,128]{3,2,1,0:T(2,128)} %trans_hbm.1) | copy-start | bytes 1941508
  4.5 0.9 %copy-start.3 = (f32[8,64,128]{2,1,0:T(8,128)S(1)}, f32[8,64,128]{2,1,0:T(8,128)}, u32[]{:S(2)}) copy-start(f32[8,64,128]{2,1,0:T(8,128)} %shift_b_hbm.1) | copy-start | bytes 786436
  5.5 0.9 %copy-start.4 = (f32[128,256]{1,0:T(8,128)S(1)}, f32[128,256]{1,0:T(8,128)}, u32[]{:S(2)}) copy-start(f32[128,256]{1,0:T(8,128)} %phi_b_hbm.1) | copy-start | bytes 393220
  6.4 0.8 %copy-start.5 = (f32[64,128]{1,0:T(8,128)S(1)}, f32[64,128]{1,0:T(8,128)}, u32[]{:S(2)}) copy-start(f32[64,128]{1,0:T(8,128)} %phi_a_hbm.1) | copy-start | bytes 98308
  7.2 0.8 %copy-start.6 = (f32[64,128]{1,0:T(8,128)S(1)}, f32[64,128]{1,0:T(8,128)}, u32[]{:S(2)}) copy-start(f32[64,128]{1,0:T(8,128)} %theta_b_hbm.1) | copy-start | bytes 98308
  7.9 0.7 copy-start.7
  8.6 0.7 copy-start.8
  9.3 0.7 copy-start.9
  10.1 0.7 copy-start.10
where the time goes:
time: 74.8 us; the launch traced here: 74.2 us
  Pallas kernels  61.7 us (82%)
  local copies, waits for them, and re-layouts  11.8 us (16%)
    pallas_call x1, Pallas kernels, on_device(): pl.pallas_call(kernel, out_shape=(jax.ShapeDtypeStruct((16, 2, 4, 4, 256)...  61.7 us
    unnamed x24, local copies, waits for them, and re-layouts  11.8 us

commit v1 on v0

--- a/solution.py
+++ b/solution.py
@@ -73,7 +73,7 @@
     pmap_hbm, list_hbm, ops_hbm, trans_hbm,
     parents_ref, incoming_ref,
     leaves, theta_a, phi_a, shift_b, theta_b, phi_b, shift_c, pmap, ilist, iops, trans,
-    q3, w3, v3, tab, acc, gains, cs,
+    q3, w3, v3, tab, middle, gains, cs,
     buf_a, recv_a, buf_b, recv_b, buf_c, recv_c, azi, group, total,
     in_sem, leaf_sem, send_a, got_a, send_b, got_b, send_c, got_c,
 ):
@@ -149,22 +149,23 @@
         pair = MERGE * jnp.concatenate([cosine, sine], 1)
         tab[o] = dot(rep_u3, jnp.concatenate(split3(pair), 0))
 
-    get_theta_b.wait()
-    pick_u = onehot(iota((64, 256), 0) == iota((64, 256), 1) // 4)
-    row = iota((512, 128), 0)
-    rep_u2 = onehot(iota((512, 128), 1) == 4 * (row // 16) + row % 4)
-    same = (iota((512, 256), 0) % 16) // 4 == iota((512, 256), 1) % 4
-    for i, half in enumerate(split(theta_b[...])):
-        wide = dot(rep_u2, dot_t(half, pick_u).astype(BF16))
-        wide = jnp.where(same, wide, 0.0).astype(BF16)
-        if i == 0:
-            v3[:, 0:256] = wide
-            v3[:, 512:768] = wide
-        else:
-            v3[:, 256:512] = wide
-
-    def compute(q):
-        def one_leaf(o, carry):
+    def middle_matrix():
+        get_theta_b.wait()
+        pick_u = onehot(iota((64, 256), 0) == iota((64, 256), 1) // 4)
+        row = iota((512, 128), 0)
+        rep_u2 = onehot(iota((512, 128), 1) == 4 * (row // 16) + row % 4)
+        same = (iota((512, 256), 0) % 16) // 4 == iota((512, 256), 1) % 4
+        for i, half in enumerate(split(theta_b[...])):
+            wide = dot(rep_u2, dot_t(half, pick_u).astype(BF16))
+            wide = jnp.where(same, wide, 0.0).astype(BF16)
+            if i == 0:
+                v3[:, 0:256] = wide
+                v3[:, 512:768] = wide
+            else:
+                v3[:, 256:512] = wide
+
+    def merge(q):
+        def one_leaf(o):
             pattern = leaves[8 * q + o].reshape(128, 128)
             hi, lo = split(pattern)
             y = dot(jnp.concatenate([hi, lo, hi], 1), q3[...])
@@ -179,48 +180,59 @@
             up = dot(w3[...], jnp.concatenate([hi, hi, lo], 0))
             cosine, sine = tab[o, :, 0:128], tab[o, :, 128:256]
             re, im = up[:, 0:128], up[:, 128:256]
-            turned = jnp.concatenate([cosine * re - sine * im, sine * re + cosine * im], 1)
-            acc[...] += turned
-            return carry
-
-        acc[...] = jnp.zeros_like(acc)
-        lax.fori_loop(0, 8, one_leaf, 0)
-        middle = acc[...]
+            middle[q, :, 0:128] += cosine * re - sine * im
+            middle[q, :, 128:256] += sine * re + cosine * im
+
+        middle[q] = jnp.zeros((256, 256), F32)
+        for o in range(8):
+            one_leaf(o)
         for c in range(2):
-            buf_a[q, :, c] = middle[:, 128 * c : 128 * c + 128].reshape(32, 8, 128)
-        hi, lo = split(middle)
+            buf_a[q, :, c] = middle[q, :, 128 * c : 128 * c + 128].reshape(32, 8, 128)
+        recv_a[4 * me + q] = buf_a[q, me]
+
+    def raise_polar(q):
+        hi, lo = split(middle[q])
         polar = dot(v3[...], jnp.concatenate([hi, hi, lo], 0))
         for c in range(2):
             buf_b[q, :, c] = polar[:, 128 * c : 128 * c + 128].reshape(32, 16, 128)
-        recv_a[4 * me + q] = buf_a[q, me]
         recv_b[4 * me + q] = buf_b[q, me]
 
-    def send(q):
-        for buf, recv, send_sem, got_sem in (
-            (buf_a, recv_a, send_a, got_a),
-            (buf_b, recv_b, send_b, got_b),
-        ):
-            for d in partners:
-                pltpu.make_async_remote_copy(
-                    src_ref=buf.at[q, d],
-                    dst_ref=recv.at[4 * me + q],
-                    send_sem=send_sem,
-                    recv_sem=got_sem,
-                    device_id={"box": d},
-                    device_id_type=MESH,
-                ).start()
+    def send(q, buf, recv, send_sem, got_sem):
+        for d in partners:
+            pltpu.make_async_remote_copy(
+                src_ref=buf.at[q, d],
+                dst_ref=recv.at[4 * me + q],
+                send_sem=send_sem,
+                recv_sem=got_sem,
+                device_id={"box": d},
+                device_id_type=MESH,
+            ).start()
+
+    def send_rows(q):
+        send(q, buf_a, recv_a, send_a, got_a)
+
+    def send_polar(q):
+        send(q, buf_b, recv_b, send_b, got_b)
 
     get_leaves[0].wait()
-    compute(0)
+    merge(0)
     pl.semaphore_wait(barrier, N - 1)
-    send(0)
+    send_rows(0)
+    middle_matrix()
+    raise_polar(0)
+    send_polar(0)
     for q in range(1, 4):
         get_leaves[q].wait()
 
     @pl.loop(1, 4)
     def _(q):
-        compute(q)
-        send(q)
+        merge(q)
+        send_rows(q)
+
+    @pl.loop(1, 4)
+    def _(q):
+        raise_polar(q)
+        send_polar(q)
 
     get_trans.wait()
     upper = iota((8, 128), 0) < 4
@@ -364,8 +376,8 @@
     return pl.pallas_call(
         kernel,
         out_shape=(
-            jax.ShapeDtypeStruct((16, 2, 4, 4, 256), F32),
-            jax.ShapeDtypeStruct((4, 2, 4, 64, 128), F32),
+            pltpu.VMEM((16, 2, 4, 4, 256), F32),
+            pltpu.VMEM((4, 2, 4, 64, 128), F32),
         ),
         in_specs=[hbm] * 11,
         out_specs=(vmem, vmem),
@@ -375,7 +387,7 @@
             pltpu.SMEM((LIST, 128), jnp.int32), pltpu.SMEM((LIST, 128), jnp.int32),
             v(2, NOPS, 2, 128),
             v(384, 256, kind=BF16), v(256, 384, kind=BF16), v(512, 768, kind=BF16),
-            v(8, 256, 256), v(256, 256), v(NOPS, 2, 8, 128), v(8, 16, 512),
+            v(8, 256, 256), v(4, 256, 256), v(NOPS, 2, 8, 128), v(8, 16, 512),
             v(4, 32, 2, 8, 128), v(128, 2, 8, 128),
             v(4, 32, 2, 16, 128), v(128, 2, 16, 128),
             v(32, 4, 2, 8, 128), v(4, 2, 256, 128),
@@ -383,7 +395,7 @@
             dma((10,)), dma((4,)), dma, dma, dma, dma, dma, dma,
         ],
         compiler_params=pltpu.CompilerParams(
-            collective_id=0, has_side_effects=True, vmem_limit_bytes=48 * 2**20
+            collective_id=0, has_side_effects=True, vmem_limit_bytes=56 * 2**20
         ),
     )(
         grid, theta_a, phi_a, shift_b, theta_b, phi_b, shift_c, parent_map.reshape(1, 128),

time: 74.8 us -> 60.2 us (0.80)
  local copies, waits for them, and re-layouts: 11.8 us -> 1.77 us
  Pallas kernels: 61.7 us -> 57.2 us
    unnamed x24 -> x2, local copies, waits for them, and re-layouts: 11.8 us -> 1.77 us
    pallas_call x1, Pallas kernels: 61.7 us -> 57.2 us  [on_device(): pl.pallas_call(kernel, out_shape=(pltpu.VMEM((16, 2, 4, 4, 256), F32), pl...]
where the time goes in v1:
time: 60.2 us; the launch traced here: 59.7 us
  Pallas kernels  57.2 us (95%)
  local copies, waits for them, and re-layouts  1.77 us (3%)
  between operations  0.64 us (1%)
    pallas_call x1, Pallas kernels, on_device(): pl.pallas_call(kernel, out_shape=(pltpu.VMEM((16, 2, 4, 4, 256), F32), pl...  57.2 us
    unnamed x2, local copies, waits for them, and re-layouts  1.77 us

profile of v1, /device:TPU:1, one launch (start us, length us, event | category | flops | bytes accessed | tf_op | source)
XLA Modules:
  0.0 59.7 jit_solution(9770663757872307021)
XLA Ops:
  0.6 57.2 %shard_map.122 = (f32[16,2,4,4,256]{4,3,2,1,0:T(4,128)S(1)}, f32[4,2,4,64,128]{4,3,2,1,0:T(8,128)S(1)}) custom-call(f32[32,2,64,128]{3,2,1,0:T(8,128)} %bitcast.8, f32[32,64]{1,0:T(8,128)} %theta_a_hbm.1, f32[64,128]{1,0:T(8,128)} %phi_a_hbm.1, f32[8,64,128]{2,1,0:T(8,128)} %shift_b_hbm.1, f32[64,128]{1,0:T(8,128)} %theta_b_hbm.1, f32[128,256]{1,0:T(8,128)} %phi_b_hbm.1, ...), custom_call_target="tpu_custom_call" | custom-call | tf_op jit(solution)/shard_map/pallas_call | solution.py:376
  57.9 0.8 %copy.16 = f32[16,2,4,4,256]{4,3,2,1,0:T(4,128)} copy(f32[16,2,4,4,256]{4,3,2,1,0:T(4,128)S(1)} %get-tuple-element.2) | data formatting | bytes 1048576
  58.7 1.0 %copy.17 = f32[4,2,4,64,128]{4,3,2,1,0:T(8,128)} copy(f32[4,2,4,64,128]{4,3,2,1,0:T(8,128)S(1)} %get-tuple-element.3) | data formatting | bytes 2097152

commit v2 on v1

--- a/solution.py
+++ b/solution.py
@@ -71,10 +71,10 @@
 def kernel(
     leaves_hbm, theta_a_hbm, phi_a_hbm, shift_b_hbm, theta_b_hbm, phi_b_hbm, shift_c_hbm,
     pmap_hbm, list_hbm, ops_hbm, trans_hbm,
-    parents_ref, incoming_ref,
+    parents_ref, recv_c,
     leaves, theta_a, phi_a, shift_b, theta_b, phi_b, shift_c, pmap, ilist, iops, trans,
     q3, w3, v3, tab, middle, gains, cs,
-    buf_a, recv_a, buf_b, recv_b, buf_c, recv_c, azi, group, total,
+    buf_a, recv_a, buf_b, recv_b, buf_c, azi, group, total,
     in_sem, leaf_sem, send_a, got_a, send_b, got_b, send_c, got_c,
 ):
     me = lax.axis_index("box")
@@ -85,26 +85,29 @@
     partners = [zs[dz] + xs[dx] + cores[dc] for dz, dx in HOPS for dc in range(2)]
     partners.append(zs[0] + xs[0] + cores[1])
 
-    barrier = pltpu.get_barrier_semaphore()
-    for d in partners:
-        pl.semaphore_signal(barrier, inc=1, device_id={"box": d}, device_id_type=MESH)
-
     def fetch(k, src, dst):
         copy = pltpu.make_async_copy(src, dst, in_sem.at[k])
         copy.start()
         return copy
 
-    get_theta_a = fetch(0, theta_a_hbm, theta_a)
-    get_phi_a = fetch(1, phi_a_hbm, phi_a)
-    get_leaves = []
-    for q in range(4):
+    def fetch_leaves(q):
         copy = pltpu.make_async_copy(
             leaves_hbm.at[pl.ds(8 * q, 8)], leaves.at[pl.ds(8 * q, 8)], leaf_sem.at[q]
         )
         copy.start()
-        get_leaves.append(copy)
+        return copy
+
     get_shift_b = fetch(2, shift_b_hbm, shift_b)
+    get_phi_a = fetch(1, phi_a_hbm, phi_a)
+    get_theta_a = fetch(0, theta_a_hbm, theta_a)
+    get_leaves = [fetch_leaves(0)]
+
+    barrier = pltpu.get_barrier_semaphore()
+    for d in partners:
+        pl.semaphore_signal(barrier, inc=1, device_id={"box": d}, device_id_type=MESH)
+
     get_theta_b = fetch(3, theta_b_hbm, theta_b)
+    get_leaves += [fetch_leaves(q) for q in range(1, 4)]
     get_trans = fetch(4, trans_hbm, trans)
     get_list = fetch(5, list_hbm, ilist)
     get_ops = fetch(6, ops_hbm, iops)
@@ -143,7 +146,7 @@
     get_shift_b.wait()
     rep_u3 = jnp.concatenate([rep_u, rep_u, rep_u], 1)
 
-    @pl.loop(0, 8)
+    @pl.loop(0, 8, unroll=True)
     def _(o):
         cosine, sine = cos_sin(shift_b[o])
         pair = MERGE * jnp.concatenate([cosine, sine], 1)
@@ -212,7 +215,7 @@
         send(q, buf_a, recv_a, send_a, got_a)
 
     def send_polar(q):
-        send(q, buf_b, recv_b, send_b, got_b)
+        send(q, buf_b, recv_b, send_b, got_b.at[q])
 
     get_leaves[0].wait()
     merge(0)
@@ -259,7 +262,8 @@
         )
 
     all_a = every(recv_a.at[pl.ds(0, 124)], send_a, got_a)
-    all_b = every(recv_b.at[pl.ds(0, 124)], send_b, got_b)
+    sent_b = every(buf_b.at[:, pl.ds(0, 31)], send_b, got_b.at[0])
+    rounds_b = [every(buf_b.at[0, pl.ds(0, 31)], send_b, got_b.at[q]) for q in range(4)]
     all_c = every(recv_c.at[:, :, pl.ds(0, 248), :], send_c, got_c)
     get_list.wait()
     get_ops.wait()
@@ -321,10 +325,8 @@
     box = iota((128, 256), 0)
     slot = iota((128, 256), 1) // 16
     total[...] = jnp.zeros_like(total)
-    all_b.wait_recv()
-
-    @pl.loop(0, 8)
-    def _(o):
+
+    def merge_octant(o):
         pick_box = onehot(box == 8 * slot + o)
         pick = jnp.where(same, dot(owner_rows, pick_box), 0.0).astype(BF16)
         rows = [
@@ -348,17 +350,31 @@
             ):
                 total[pl.ds(8 * h, 8), c] += turned
 
+    for q in range(4):
+        rounds_b[q].wait_recv()
+        merge_octant(q)
+        merge_octant(q + 4)
+
     for i in range(4):
         parents_ref[:, :, i] = total[:, :, 4 * i : 4 * i + 4, :]
 
     all_c.wait_recv()
+    all_a.wait_send()
+    sent_b.wait_send()
+    all_c.wait_send()
+
+
+def write(parents_in, rows_in, parents_hbm, incoming_hbm, rows, sem):
+    copies = [pltpu.make_async_copy(parents_in, parents_hbm, sem.at[4])]
+    copies[0].start()
     for k in range(4):
         for c in range(2):
             for i in range(4):
-                incoming_ref[k, c, i] = recv_c[k, c, pl.ds(i, 64, stride=4), :]
-    all_a.wait_send()
-    all_b.wait_send()
-    all_c.wait_send()
+                rows[k, c, i] = rows_in[k, c, pl.ds(i, 64, stride=4), :]
+        copies.append(pltpu.make_async_copy(rows.at[k], incoming_hbm.at[k], sem.at[k]))
+        copies[-1].start()
+    for copy in copies:
+        copy.wait()
 
 
 def on_device(
@@ -373,11 +389,11 @@
         return pltpu.VMEM(shape, kind)
 
     dma = pltpu.SemaphoreType.DMA
-    return pl.pallas_call(
+    parents, rows = pl.pallas_call(
         kernel,
         out_shape=(
             pltpu.VMEM((16, 2, 4, 4, 256), F32),
-            pltpu.VMEM((4, 2, 4, 64, 128), F32),
+            pltpu.VMEM((4, 2, 256, 128), F32),
         ),
         in_specs=[hbm] * 11,
         out_specs=(vmem, vmem),
@@ -390,9 +406,9 @@
             v(8, 256, 256), v(4, 256, 256), v(NOPS, 2, 8, 128), v(8, 16, 512),
             v(4, 32, 2, 8, 128), v(128, 2, 8, 128),
             v(4, 32, 2, 16, 128), v(128, 2, 16, 128),
-            v(32, 4, 2, 8, 128), v(4, 2, 256, 128),
+            v(32, 4, 2, 8, 128),
             v(384, 256, kind=BF16), v(512, 128), v(16, 2, 16, 256),
-            dma((10,)), dma((4,)), dma, dma, dma, dma, dma, dma,
+            dma((10,)), dma((4,)), dma, dma, dma, dma((4,)), dma, dma,
         ],
         compiler_params=pltpu.CompilerParams(
             collective_id=0, has_side_effects=True, vmem_limit_bytes=56 * 2**20
@@ -401,6 +417,17 @@
         grid, theta_a, phi_a, shift_b, theta_b, phi_b, shift_c, parent_map.reshape(1, 128),
         inter_list.T, op_index.T, trans_ops,
     )
+    return pl.pallas_call(
+        write,
+        out_shape=(
+            jax.ShapeDtypeStruct((16, 2, 4, 4, 256), F32),
+            jax.ShapeDtypeStruct((4, 2, 4, 64, 128), F32),
+        ),
+        in_specs=[vmem, vmem],
+        out_specs=(hbm, hbm),
+        scratch_shapes=[v(4, 2, 4, 64, 128), dma((5,))],
+        compiler_params=pltpu.CompilerParams(vmem_limit_bytes=8 * 2**20),
+    )(parents, rows)
 
 
 def solution(mesh):

time: 60.2 us -> 57.3 us (0.952)
  local copies, waits for them, and re-layouts: 1.77 us -> 0 us
    pallas_call x1, Pallas kernels: 57.2 us -> 55.4 us  [on_device(): pl.pallas_call(kernel, out_shape=(pltpu.VMEM((16, 2, 4, 4, 256), F32), pl...]
    unnamed x2 -> x0, local copies, waits for them, and re-layouts: 1.77 us -> none
    pallas_call x0 -> x1, Pallas kernels: none -> 1.18 us  [on_device(): pl.pallas_call(write, out_shape=(jax.ShapeDtypeStruct((16, 2, 4, 4, 256),...]
where the time goes in v2:
time: 57.3 us; the launch traced here: 57.2 us
  Pallas kernels  56.6 us (99%)
  between operations  0.64 us (1%)
    pallas_call x1, Pallas kernels, on_device(): pl.pallas_call(kernel, out_shape=(pltpu.VMEM((16, 2, 4, 4, 256), F32), pl...  55.4 us
    pallas_call x1, Pallas kernels, on_device(): pl.pallas_call(write, out_shape=(jax.ShapeDtypeStruct((16, 2, 4, 4, 256),...  1.18 us

profile of v2, /device:TPU:1, one launch (start us, length us, event | category | flops | bytes accessed | tf_op | source)
XLA Modules:
  0.0 57.2 jit_solution(6408745120576018756)
XLA Ops:
  0.6 55.4 %shard_map.122 = (f32[16,2,4,4,256]{4,3,2,1,0:T(4,128)S(1)}, f32[4,2,256,128]{3,2,1,0:T(8,128)S(1)}) custom-call(f32[32,2,64,128]{3,2,1,0:T(8,128)} %bitcast.8, f32[32,64]{1,0:T(8,128)} %theta_a_hbm.1, f32[64,128]{1,0:T(8,128)} %phi_a_hbm.1, f32[8,64,128]{2,1,0:T(8,128)} %shift_b_hbm.1, f32[64,128]{1,0:T(8,128)} %theta_b_hbm.1, f32[128,256]{1,0:T(8,128)} %phi_b_hbm.1, ...), custom_call_target="tpu_custom_call" | custom-call | tf_op jit(solution)/shard_map/pallas_call | solution.py:392
  56.0 1.2 %shard_map.123 = (f32[16,2,4,4,256]{4,3,2,1,0:T(4,128)}, f32[4,2,4,64,128]{4,3,2,1,0:T(8,128)}) custom-call(f32[16,2,4,4,256]{4,3,2,1,0:T(4,128)S(1)} %get-tuple-element.4.parents_in, f32[4,2,256,128]{3,2,1,0:T(8,128)S(1)} %get-tuple-element.5.rows_in), custom_call_target="tpu_custom_call" | custom-call | tf_op jit(solution)/shard_map/pallas_call | solution.py:420

commit v3 on v2

--- a/solution.py
+++ b/solution.py
@@ -23,6 +23,8 @@
     (1, 1), (3, 3),
     (0, 1), (0, 3), (1, 0), (3, 0),
 )
+
+OFFSETS = tuple((dz, dx, dc) for dz, dx in HOPS for dc in range(2)) + ((0, 0, 1),)
 
 
 def dot(a, b):
@@ -74,16 +76,30 @@
     parents_ref, recv_c,
     leaves, theta_a, phi_a, shift_b, theta_b, phi_b, shift_c, pmap, ilist, iops, trans,
     q3, w3, v3, tab, middle, gains, cs,
-    buf_a, recv_a, buf_b, recv_b, buf_c, azi, group, total,
-    in_sem, leaf_sem, send_a, got_a, send_b, got_b, send_c, got_c,
+    buf_a, held_a, recv_a, buf_b, held_b, recv_b, buf_c, azi, group, total,
+    in_sem, leaf_sem, send_held, got_held, send_a, got_a, send_b, got_b, send_c, got_c,
 ):
     me = lax.axis_index("box")
     z, x, core = me // 8, (me // 2) % 4, me % 2
     zs = [((z + k) % 4) * 8 for k in range(4)]
     xs = [((x + k) % 4) * 2 for k in range(4)]
     cores = [core, 1 - core]
-    partners = [zs[dz] + xs[dx] + cores[dc] for dz, dx in HOPS for dc in range(2)]
-    partners.append(zs[0] + xs[0] + cores[1])
+
+    def device(dz, dx, dc):
+        return zs[dz] + xs[dx] + cores[dc]
+
+    partners = [device(*offset) for offset in OFFSETS]
+    relays, origins, near, far = [], [], [], []
+    for q in range(4):
+        axis, step = ((0, 1), (1, 3), (0, 3), (1, 1))[q]
+        ahead = [0, 0, 0]
+        ahead[axis] = step
+        behind = [0, 0, 0]
+        behind[axis] = 4 - step
+        relays.append(device(*ahead))
+        origins.append(device(*behind))
+        near.append([device(*offset) for offset in OFFSETS if offset[axis] in (0, 4 - step)])
+        far.append([device(*offset) for offset in OFFSETS if offset[axis] in (0, step)])
 
     def fetch(k, src, dst):
         copy = pltpu.make_async_copy(src, dst, in_sem.at[k])
@@ -193,49 +209,72 @@
             buf_a[q, :, c] = middle[q, :, 128 * c : 128 * c + 128].reshape(32, 8, 128)
         recv_a[4 * me + q] = buf_a[q, me]
 
-    def raise_polar(q):
-        hi, lo = split(middle[q])
+    def raise_polar(q, rows, raised, origin):
+        both = [rows[q, :, c].reshape(256, 128) for c in range(2)]
+        hi, lo = split(jnp.concatenate(both, 1))
         polar = dot(v3[...], jnp.concatenate([hi, hi, lo], 0))
         for c in range(2):
-            buf_b[q, :, c] = polar[:, 128 * c : 128 * c + 128].reshape(32, 16, 128)
-        recv_b[4 * me + q] = buf_b[q, me]
-
-    def send(q, buf, recv, send_sem, got_sem):
-        for d in partners:
+            raised[q, :, c] = polar[:, 128 * c : 128 * c + 128].reshape(32, 16, 128)
+        recv_b[4 * origin + q] = raised[q, me]
+
+    def send(buf, origin, q, targets, recv, send_sem, got_sem):
+        for d in targets:
             pltpu.make_async_remote_copy(
                 src_ref=buf.at[q, d],
-                dst_ref=recv.at[4 * me + q],
+                dst_ref=recv.at[4 * origin + q],
                 send_sem=send_sem,
                 recv_sem=got_sem,
                 device_id={"box": d},
                 device_id_type=MESH,
             ).start()
 
-    def send_rows(q):
-        send(q, buf_a, recv_a, send_a, got_a)
-
-    def send_polar(q):
-        send(q, buf_b, recv_b, send_b, got_b.at[q])
-
-    get_leaves[0].wait()
-    merge(0)
-    pl.semaphore_wait(barrier, N - 1)
-    send_rows(0)
-    middle_matrix()
-    raise_polar(0)
-    send_polar(0)
-    for q in range(1, 4):
+    hand_on = [
+        pltpu.make_async_remote_copy(
+            src_ref=buf_a.at[q],
+            dst_ref=held_a.at[q],
+            send_sem=send_held.at[q],
+            recv_sem=got_held.at[q],
+            device_id={"box": relays[q]},
+            device_id_type=MESH,
+        )
+        for q in range(4)
+    ]
+
+    def near_polar(q):
+        raise_polar(q, buf_a, buf_b, me)
+        send(buf_b, me, q, near[q], recv_b, send_b, got_b.at[q])
+
+    for q in range(4):
         get_leaves[q].wait()
-
-    @pl.loop(1, 4)
-    def _(q):
         merge(q)
-        send_rows(q)
-
-    @pl.loop(1, 4)
-    def _(q):
-        raise_polar(q)
-        send_polar(q)
+        if q == 0:
+            pl.semaphore_wait(barrier, N - 1)
+        hand_on[q].start()
+        send(buf_a, me, q, near[q], recv_a, send_a, got_a)
+        if q == 0:
+            middle_matrix()
+            near_polar(0)
+
+    def far_rows(q):
+        hand_on[q].wait_recv()
+        send(held_a, origins[q], q, far[q], recv_a, send_a, got_a)
+        recv_a[4 * origins[q] + q] = held_a[q, me]
+
+    def far_polar(q):
+        raise_polar(q, held_a, held_b, origins[q])
+        send(held_b, origins[q], q, far[q], recv_b, send_b, got_b.at[q])
+
+    far_rows(0)
+    near_polar(1)
+    far_rows(1)
+    near_polar(2)
+    far_rows(2)
+    far_polar(0)
+    far_rows(3)
+    far_polar(1)
+    near_polar(3)
+    far_polar(2)
+    far_polar(3)
 
     get_trans.wait()
     upper = iota((8, 128), 0) < 4
@@ -261,9 +300,9 @@
             device_id_type=MESH,
         )
 
-    all_a = every(recv_a.at[pl.ds(0, 124)], send_a, got_a)
-    sent_b = every(buf_b.at[:, pl.ds(0, 31)], send_b, got_b.at[0])
-    rounds_b = [every(buf_b.at[0, pl.ds(0, 31)], send_b, got_b.at[q]) for q in range(4)]
+    all_a = every(recv_a.at[pl.ds(0, 120)], send_a, got_a)
+    sent_b = every(buf_b.at[:, pl.ds(0, 30)], send_b, got_b.at[0])
+    rounds_b = [every(buf_b.at[0, pl.ds(0, 30)], send_b, got_b.at[q]) for q in range(4)]
     all_c = every(recv_c.at[:, :, pl.ds(0, 248), :], send_c, got_c)
     get_list.wait()
     get_ops.wait()
@@ -359,6 +398,8 @@
         parents_ref[:, :, i] = total[:, :, 4 * i : 4 * i + 4, :]
 
     all_c.wait_recv()
+    for q in range(4):
+        hand_on[q].wait_send()
     all_a.wait_send()
     sent_b.wait_send()
     all_c.wait_send()
@@ -404,11 +445,11 @@
             v(2, NOPS, 2, 128),
             v(384, 256, kind=BF16), v(256, 384, kind=BF16), v(512, 768, kind=BF16),
             v(8, 256, 256), v(4, 256, 256), v(NOPS, 2, 8, 128), v(8, 16, 512),
-            v(4, 32, 2, 8, 128), v(128, 2, 8, 128),
-            v(4, 32, 2, 16, 128), v(128, 2, 16, 128),
+            v(4, 32, 2, 8, 128), v(4, 32, 2, 8, 128), v(128, 2, 8, 128),
+            v(4, 32, 2, 16, 128), v(4, 32, 2, 16, 128), v(128, 2, 16, 128),
             v(32, 4, 2, 8, 128),
             v(384, 256, kind=BF16), v(512, 128), v(16, 2, 16, 256),
-            dma((10,)), dma((4,)), dma, dma, dma, dma((4,)), dma, dma,
+            dma((10,)), dma((4,)), dma((4,)), dma((4,)), dma, dma, dma, dma((4,)), dma, dma,
         ],
         compiler_params=pltpu.CompilerParams(
             collective_id=0, has_side_effects=True, vmem_limit_bytes=56 * 2**20

time: 57.3 us -> 55.8 us (0.974)
  Pallas kernels: 56.6 us -> 54.9 us
    pallas_call x1, Pallas kernels: 55.4 us -> 53.7 us  [on_device(): pl.pallas_call(kernel, out_shape=(pltpu.VMEM((16, 2, 4, 4, 256), F32), pl...]
where the time goes in v3:
time: 55.8 us; the launch traced here: 55.7 us
  Pallas kernels  54.9 us (98%)
  between operations  0.8 us (1%)
    pallas_call x1, Pallas kernels, on_device(): pl.pallas_call(kernel, out_shape=(pltpu.VMEM((16, 2, 4, 4, 256), F32), pl...  53.7 us
    pallas_call x1, Pallas kernels, on_device(): pl.pallas_call(write, out_shape=(jax.ShapeDtypeStruct((16, 2, 4, 4, 256),...  1.18 us

profile of v3, /device:TPU:1, one launch (start us, length us, event | category | flops | bytes accessed | tf_op | source)
XLA Modules:
  0.0 55.7 jit_solution(16620373295516180349)
XLA Ops:
  0.6 53.7 %shard_map.122 = (f32[16,2,4,4,256]{4,3,2,1,0:T(4,128)S(1)}, f32[4,2,256,128]{3,2,1,0:T(8,128)S(1)}) custom-call(f32[32,2,64,128]{3,2,1,0:T(8,128)} %bitcast.8, f32[32,64]{1,0:T(8,128)} %theta_a_hbm.1, f32[64,128]{1,0:T(8,128)} %phi_a_hbm.1, f32[8,64,128]{2,1,0:T(8,128)} %shift_b_hbm.1, f32[64,128]{1,0:T(8,128)} %theta_b_hbm.1, f32[128,256]{1,0:T(8,128)} %phi_b_hbm.1, ...), custom_call_target="tpu_custom_call" | custom-call | tf_op jit(solution)/shard_map/pallas_call | solution.py:433
  54.4 1.2 %shard_map.123 = (f32[16,2,4,4,256]{4,3,2,1,0:T(4,128)}, f32[4,2,4,64,128]{4,3,2,1,0:T(8,128)}) custom-call(f32[16,2,4,4,256]{4,3,2,1,0:T(4,128)S(1)} %get-tuple-element.4.parents_in, f32[4,2,256,128]{3,2,1,0:T(8,128)S(1)} %get-tuple-element.5.rows_in), custom_call_target="tpu_custom_call" | custom-call | tf_op jit(solution)/shard_map/pallas_call | solution.py:461

commit v4 on v3

--- a/solution.py
+++ b/solution.py
@@ -81,8 +81,9 @@
 ):
     me = lax.axis_index("box")
     z, x, core = me // 8, (me // 2) % 4, me % 2
-    zs = [((z + k) % 4) * 8 for k in range(4)]
-    xs = [((x + k) % 4) * 2 for k in range(4)]
+    sign = 1 - 2 * core
+    zs = [((z + 4 + sign * k) % 4) * 8 for k in range(4)]
+    xs = [((x + 4 + sign * k) % 4) * 2 for k in range(4)]
     cores = [core, 1 - core]
 
     def device(dz, dx, dc):

time: 55.8 us -> 56 us (level)
  no operation moved by 1% of the time
where the time goes in v4:
time: 56 us; the launch traced here: 55.9 us
  Pallas kernels  55.1 us (98%)
  between operations  0.8 us (1%)
    pallas_call x1, Pallas kernels, on_device(): pl.pallas_call(kernel, out_shape=(pltpu.VMEM((16, 2, 4, 4, 256), F32), pl...  53.9 us
    pallas_call x1, Pallas kernels, on_device(): pl.pallas_call(write, out_shape=(jax.ShapeDtypeStruct((16, 2, 4, 4, 256),...  1.18 us

profile of v4, /device:TPU:1, one launch (start us, length us, event | category | flops | bytes accessed | tf_op | source)
XLA Modules:
  0.0 55.9 jit_solution(146979984427829301)
XLA Ops:
  0.6 53.9 %shard_map.122 = (f32[16,2,4,4,256]{4,3,2,1,0:T(4,128)S(1)}, f32[4,2,256,128]{3,2,1,0:T(8,128)S(1)}) custom-call(f32[32,2,64,128]{3,2,1,0:T(8,128)} %bitcast.8, f32[32,64]{1,0:T(8,128)} %theta_a_hbm.1, f32[64,128]{1,0:T(8,128)} %phi_a_hbm.1, f32[8,64,128]{2,1,0:T(8,128)} %shift_b_hbm.1, f32[64,128]{1,0:T(8,128)} %theta_b_hbm.1, f32[128,256]{1,0:T(8,128)} %phi_b_hbm.1, ...), custom_call_target="tpu_custom_call" | custom-call | tf_op jit(solution)/shard_map/pallas_call | solution.py:434
  54.6 1.2 %shard_map.123 = (f32[16,2,4,4,256]{4,3,2,1,0:T(4,128)}, f32[4,2,4,64,128]{4,3,2,1,0:T(8,128)}) custom-call(f32[16,2,4,4,256]{4,3,2,1,0:T(4,128)S(1)} %get-tuple-element.4.parents_in, f32[4,2,256,128]{3,2,1,0:T(8,128)S(1)} %get-tuple-element.5.rows_in), custom_call_target="tpu_custom_call" | custom-call | tf_op jit(solution)/shard_map/pallas_call | solution.py:462
